TPU v7x, 128 devices: a whole 4x4x4 slice. The times are simulated.
128 devices in a mesh: dp: 4 (over x), expert: 32 (over z, y, core).
Axes of the slice: x: 4, y: 4, z: 4, core: 2. Of those that a mesh axis runs over, the one named last changes fastest.
Arguments:
- tokens: bfloat16 [16384, 2048], P(('dp', 'expert')), may hold values from -6 to 6
- expert_ids: int32 [16384, 4], P(('dp', 'expert')), may hold values from 0 to 63, all different within a row; in each aligned block of 128 rows (0 to 127, 128 to 255, ...) at most 14 rows name the same one
- gate_weights: float32 [16384, 4], P(('dp', 'expert')), may hold values from 0.05 to 0.5
- slot_of_expert: int32 [64], replicated, may hold values from 0 to 63, each once
- w_gate: bfloat16 [64, 2048, 768], P('expert'), may hold values from -0.125 to 0.125
- w_up: bfloat16 [64, 2048, 768], P('expert'), may hold values from -0.125 to 0.125
- w_down: bfloat16 [64, 768, 2048], P('expert'), may hold values from -0.21875 to 0.21875
- d_out: bfloat16 [16384, 2048], P(('dp', 'expert')), may hold values from -6 to 6
Outputs:
- layer_out: bfloat16 [16384, 2048], P(('dp', 'expert'))
- d_tokens: bfloat16 [16384, 2048], P(('dp', 'expert'))
- d_gates: float32 [16384, 4], P(('dp', 'expert'))
- grad_gate: bfloat16 [64, 2048, 768], P('expert', 'dp')
- grad_up: bfloat16 [64, 2048, 768], P('expert', 'dp')
- grad_down: bfloat16 [64, 768, 2048], P('expert', None, 'dp')
Inputs may be any that keep to these rules, and one draw needn't show every extreme that they name: `expert_ids`: each row names 4 different experts. Among the 128 rows of one device (aligned blocks of rows) no expert is named more than 14 times, and in every draw some expert is named exactly 14 times in some block. A permutation: expert e's weights stand at index slot_of_expert[e] of w_gate, w_up and w_down, and its gradients at that index of the outputs.
All inputs are finite; a program needn't handle non-finite values.
Results may differ from a plain program's by a relative error of at most 0.0095.
Values may be sent and summed in bfloat16 or wider, within the bound.
A program may use at most 192 MiB of HBM per device.

v0:
```python
import jax
import jax.numpy as jnp
from jax import lax
from jax.sharding import PartitionSpec as P


def on_device(tokens, expert_ids, gate_weights, slot_of_expert, w_gate, w_up, w_down, d_out):
    peer_count = lax.axis_size("expert")
    local_count = w_gate.shape[0]
    experts_all = local_count * peer_count
    tok_rows = tokens.shape[0]
    top_count = expert_ids.shape[1]
    width = tokens.shape[1]
    capacity = tok_rows * top_count * 7 // (4 * experts_all)
    spot_count = experts_all * capacity
    expert_range = jnp.arange(experts_all, dtype=jnp.int32)
    slot_ids = jnp.sum(jnp.where(expert_ids[:, :, None] == expert_range, slot_of_expert, 0), axis=2)
    flat_slots = slot_ids.reshape(-1)
    onehot = (flat_slots[:, None] == expert_range).astype(jnp.int32)
    ranks = jnp.sum((jnp.cumsum(onehot, axis=0) - 1) * onehot, axis=1)
    position = (flat_slots * capacity + ranks).reshape(tok_rows, top_count)
    spot_range = jnp.arange(spot_count, dtype=jnp.int32)
    picked = position[None, :, :] == spot_range[:, None, None]
    dispatch = jnp.any(picked, axis=2).astype(jnp.bfloat16)
    gate_spot = jnp.sum(jnp.where(picked, gate_weights[None, :, :], 0.0), axis=(1, 2))
    send_rows = jnp.dot(dispatch, tokens, preferred_element_type=jnp.float32).astype(jnp.bfloat16)
    send_rows = send_rows.reshape(peer_count, local_count, capacity, width)
    received = lax.all_to_all(send_rows, "expert", split_axis=0, concat_axis=0, tiled=True)
    pre_gate = jnp.einsum("pecd,edf->pecf", received, w_gate, preferred_element_type=jnp.float32)
    pre_up = jnp.einsum("pecd,edf->pecf", received, w_up, preferred_element_type=jnp.float32)
    hidden = (pre_gate * jax.nn.sigmoid(pre_gate) * pre_up).astype(jnp.bfloat16)
    outputs = jnp.einsum(
        "pecf,efd->pecd", hidden, w_down, preferred_element_type=jnp.float32
    ).astype(jnp.bfloat16)
    returned = lax.all_to_all(outputs, "expert", split_axis=0, concat_axis=0, tiled=True)
    results = (returned, pre_gate, pre_up)
    returned = results[0].reshape(spot_count, width)
    gathered = jnp.einsum(
        "srk,sd->krd", picked.astype(jnp.bfloat16), returned, preferred_element_type=jnp.float32
    )
    layer_out = jnp.sum(gate_weights.T[:, :, None] * gathered, axis=0).astype(jnp.bfloat16)
    d_gates = jnp.sum(d_out.astype(jnp.float32)[None, :, :] * gathered, axis=2).T
    d_spots = jnp.dot(dispatch, d_out, preferred_element_type=jnp.float32)
    d_send = (
        (gate_spot[:, None] * d_spots)
        .astype(jnp.bfloat16)
        .reshape(peer_count, local_count, capacity, width)
    )
    pre_gate, pre_up = (results[1], results[2])
    kept_rows, d_rows = (
        lax.all_to_all(send_rows, "expert", split_axis=0, concat_axis=0, tiled=True),
        lax.all_to_all(d_send, "expert", split_axis=0, concat_axis=0, tiled=True),
    )
    sigma = jax.nn.sigmoid(pre_gate)
    silu_gate = pre_gate * sigma
    hidden = (silu_gate * pre_up).astype(jnp.bfloat16)
    d_hidden = jnp.einsum("pecd,efd->pecf", d_rows, w_down, preferred_element_type=jnp.float32)
    d_gate_pre = (d_hidden * pre_up * sigma * (1.0 + pre_gate * (1.0 - sigma))).astype(jnp.bfloat16)
    d_up_pre = (d_hidden * silu_gate).astype(jnp.bfloat16)
    d_inputs = jnp.einsum("pecf,edf->pecd", d_gate_pre, w_gate, preferred_element_type=jnp.float32)
    d_inputs = d_inputs + jnp.einsum(
        "pecf,edf->pecd", d_up_pre, w_up, preferred_element_type=jnp.float32
    )
    d_back = lax.all_to_all(
        d_inputs.astype(jnp.bfloat16), "expert", split_axis=0, concat_axis=0, tiled=True
    )
    d_tokens = jnp.dot(
        dispatch.T, d_back.reshape(spot_count, width), preferred_element_type=jnp.float32
    ).astype(jnp.bfloat16)
    term_gate = jnp.einsum(
        "pecd,pecf->edf", kept_rows, d_gate_pre, preferred_element_type=jnp.float32
    )
    term_up = jnp.einsum("pecd,pecf->edf", kept_rows, d_up_pre, preferred_element_type=jnp.float32)
    term_down = jnp.einsum("pecf,pecd->efd", hidden, d_rows, preferred_element_type=jnp.float32)
    sum_gate, sum_up, sum_down = (
        lax.psum_scatter(
            term_gate.astype(jnp.bfloat16), "dp", scatter_dimension=1, tiled=True
        ).astype(jnp.float32),
        lax.psum_scatter(
            term_up.astype(jnp.bfloat16), "dp", scatter_dimension=1, tiled=True
        ).astype(jnp.float32),
        lax.psum_scatter(
            term_down.astype(jnp.bfloat16), "dp", scatter_dimension=2, tiled=True
        ).astype(jnp.float32),
    )
    return (
        layer_out,
        d_tokens,
        d_gates,
        sum_gate.astype(jnp.bfloat16),
        sum_up.astype(jnp.bfloat16),
        sum_down.astype(jnp.bfloat16),
    )


def solution(mesh):
    in_specs = (
        P(("dp", "expert"), None),
        P(("dp", "expert"), None),
        P(("dp", "expert"), None),
        P(),
        P("expert", None, None),
        P("expert", None, None),
        P("expert", None, None),
        P(("dp", "expert"), None),
    )
    out_specs = (
        P(("dp", "expert"), None),
        P(("dp", "expert"), None),
        P(("dp", "expert"), None),
        P("expert", "dp", None),
        P("expert", "dp", None),
        P("expert", None, "dp"),
    )
    return jax.shard_map(
        on_device, mesh=mesh, in_specs=in_specs, out_specs=out_specs, check_vma=False
    )
```

profile of v0, /device:TPU:1, one launch (start us, length us, event | category | flops | bytes accessed | tf_op | source)
XLA Modules:
  0.0 366.0 jit_solution(17164005954346817103)
XLA Ops:
  10.5 2.9 convolution_convert_fusion
  13.4 6.0 %reshape.58 = bf16[32,2,14,2048]{3,2,1,0:T(8,128)(2,1)} reshape(bf16[896,2048]{1,0:T(8,128)(2,1)} %convolution_convert_fusion) | data formatting | bytes 7340032 | tf_op jit(solution)/shard_map/reshape | solution.py:27
  19.4 7.8 %copy.64 = bf16[32,2,14,2048]{3,1,2,0:T(2,128)(2,1)} copy(bf16[32,2,14,2048]{3,2,1,0:T(8,128)(2,1)} %reshape.58) | data formatting | bytes 7340032 | tf_op jit(solution)/shard_map/reshape | solution.py:27
  27.3 10.3 %all-to-all-start = ((bf16[32,2,14,2048]{3,1,2,0:T(2,128)(2,1)}), bf16[32,2,14,2048]{3,1,2,0:T(2,128)(2,1)}, u32[]{:S(2)}, u32[]{:S(2)}) async-start(bf16[32,2,14,2048]{3,1,2,0:T(2,128)(2,1)} %copy.64), calls=%async_computation | async-start | bytes 7340032 | tf_op jit(solution)/shard_map/all_to_all | solution.py:28
  37.8 3.0 multiply_convert_fusion
  40.8 6.0 %reshape.60 = bf16[32,2,14,2048]{3,2,1,0:T(8,128)(2,1)} reshape(bf16[896,2048]{1,0:T(8,128)(2,1)} %multiply_convert_fusion) | data formatting | bytes 7340032 | tf_op jit(solution)/shard_map/reshape | solution.py:47
  46.9 7.9 %copy.70 = bf16[32,2,14,2048]{3,1,2,0:T(2,128)(2,1)} copy(bf16[32,2,14,2048]{3,2,1,0:T(8,128)(2,1)} %reshape.60) | data formatting | bytes 7340032 | tf_op jit(solution)/shard_map/reshape | solution.py:47
  54.8 27.7 %all-to-all-done = bf16[32,2,14,2048]{3,1,2,0:T(2,128)(2,1)} async-done(((bf16[32,2,14,2048]{3,1,2,0:T(2,128)(2,1)}), bf16[32,2,14,2048]{3,1,2,0:T(2,128)(2,1)}, u32[]{:S(2)}, u32[]{:S(2)}) %all-to-all-start) | async-done | bytes 3670048 | tf_op jit(solution)/shard_map/all_to_all | solution.py:28
  82.5 7.2 %all-to-all-start.2 = ((bf16[32,2,14,2048]{3,1,2,0:T(2,128)(2,1)}), bf16[32,2,14,2048]{3,1,2,0:T(2,128)(2,1)}, u32[]{:S(2)}, u32[]{:S(2)}) async-start(bf16[32,2,14,2048]{3,1,2,0:T(2,128)(2,1)} %copy.70), calls=%async_computation.2 | async-start | bytes 7340032 | tf_op jit(solution)/shard_map/all_to_all | solution.py:52
  90.3 10.9 %fusion.2 = f32[2,32,14,768]{3,1,2,0:T(8,128)} fusion(bf16[2,2048,768]{2,1,0:T(8,128)(2,1)} %param.13, bf16[32,2,14,2048]{3,1,2,0:T(2,128)(2,1)} %all-to-all-done), kind=kOutput, calls=%fused_computation.7 | convolution fusion | flops 2818572288 | bytes 12713984 | tf_op jit(solution)/shard_map/pecd,edf->pecf/dot_general | solution.py:30
  101.2 11.0 %fusion.6 = f32[2,32,14,768]{3,1,2,0:T(8,128)} fusion(bf16[2,2048,768]{2,1,0:T(8,128)(2,1)} %param.12, bf16[32,2,14,2048]{3,1,2,0:T(2,128)(2,1)} %all-to-all-done), kind=kOutput, calls=%fused_computation.11 | convolution fusion | flops 2818572288 | bytes 12713984 | tf_op jit(solution)/shard_map/pecd,edf->pecf/dot_general | solution.py:29
  112.2 22.8 %all-to-all-done.2 = bf16[32,2,14,2048]{3,1,2,0:T(2,128)(2,1)} async-done(((bf16[32,2,14,2048]{3,1,2,0:T(2,128)(2,1)}), bf16[32,2,14,2048]{3,1,2,0:T(2,128)(2,1)}, u32[]{:S(2)}, u32[]{:S(2)}) %all-to-all-start.2) | async-done | bytes 3670048 | tf_op jit(solution)/shard_map/all_to_all | solution.py:52
  135.0 13.4 %fusion.25 = (bf16[32,2,14,768]{3,0,2,1:T(8,128)(2,1)S(1)}, bf16[32,2,14,768]{3,0,2,1:T(8,128)(2,1)S(1)}, bf16[32,2,14,768]{3,0,2,1:T(8,128)(2,1)}) fusion(f32[2,32,14,768]{3,1,2,0:T(8,128)} %fusion.2, f32[2,32,14,768]{3,1,2,0:T(8,128)} %fusion.6, bf16[2,768,2048]{2,1,0:T(8,128)(2,1)} %param.14, bf16[32,2,14,2048]{3,1,2,0:T(2,128)(2,1)} %all-to-all-done.2), kind=kOutput, calls=%fused_computation.32 | convolution fusion | flops 2828894208 | bytes 19595264 | tf_op jit(solution)/shard_map/pecd,efd->pecf/dot_general | solution.py:57
  149.5 13.3 %bitcast_convert_fusion = bf16[2,768,2048]{2,1,0:T(8,128)(2,1)} fusion(bf16[32,2,14,768]{3,0,2,1:T(8,128)(2,1)S(1)} %get-tuple-element.27, bf16[32,2,14,2048]{3,1,2,0:T(2,128)(2,1)} %all-to-all-done.2), kind=kOutput, calls=%fused_computation | convolution fusion | flops 2821718016 | bytes 11337728 | tf_op jit(solution)/shard_map/pecf,pecd->efd/dot_general | solution.py:74
  163.0 11.8 %bitcast_convert_fusion.2 = bf16[2,2048,768]{2,1,0:T(8,128)(2,1)} fusion(bf16[32,2,14,768]{3,0,2,1:T(8,128)(2,1)S(1)} %get-tuple-element.26, bf16[32,2,14,2048]{3,1,2,0:T(2,128)(2,1)} %all-to-all-done), kind=kOutput, calls=%fused_computation.2 | convolution fusion | flops 2821718016 | bytes 11337728 | tf_op jit(solution)/shard_map/pecd,pecf->edf/dot_general | solution.py:70
  175.3 12.2 %bitcast_convert_fusion.1 = bf16[2,2048,768]{2,1,0:T(8,128)(2,1)} fusion(bf16[32,2,14,768]{3,0,2,1:T(8,128)(2,1)} %get-tuple-element.28, bf16[32,2,14,2048]{3,1,2,0:T(2,128)(2,1)} %all-to-all-done), kind=kOutput, calls=%fused_computation.1 | convolution fusion | flops 2821718016 | bytes 11337728 | tf_op jit(solution)/shard_map/pecd,pecf->edf/dot_general | solution.py:73
  187.6 6.3 %convert_bitcast_fusion = bf16[32,2,14,2048]{3,0,2,1:T(8,128)(2,1)S(1)} fusion(bf16[32,2,14,768]{3,0,2,1:T(8,128)(2,1)} %copy-done.4, bf16[2,768,2048]{2,1,0:T(8,128)(2,1)} %param.14), kind=kOutput, calls=%fused_computation.24 | convolution fusion | flops 2820407296 | bytes 11337728 | tf_op jit(solution)/shard_map/pecf,efd->pecd/dot_general | solution.py:32
  193.9 5.7 %copy.67 = bf16[32,2,14,2048]{3,1,2,0:T(2,128)(2,1)} copy(bf16[32,2,14,2048]{3,0,2,1:T(8,128)(2,1)S(1)} %convert_bitcast_fusion) | data formatting | bytes 7340032 | tf_op jit(solution)/shard_map/convert_element_type | solution.py:34
  199.6 7.3 %all-to-all-start.1 = ((bf16[32,2,14,2048]{3,1,2,0:T(2,128)(2,1)}), bf16[32,2,14,2048]{3,1,2,0:T(2,128)(2,1)}, u32[]{:S(2)}, u32[]{:S(2)}) async-start(bf16[32,2,14,2048]{3,1,2,0:T(2,128)(2,1)} %copy.67), calls=%async_computation.1 | async-start | bytes 7340032 | tf_op jit(solution)/shard_map/all_to_all | solution.py:35
  207.0 9.2 %fusion = f32[2,32,14,2048]{3,1,2,0:T(8,128)} fusion(bf16[32,2,14,768]{3,0,2,1:T(8,128)(2,1)} %get-tuple-element.28, bf16[2,2048,768]{2,1,0:T(8,128)(2,1)} %param.13), kind=kOutput, calls=%fused_computation.5 | convolution fusion | flops 2818572288 | bytes 15007744 | tf_op jit(solution)/shard_map/pecf,edf->pecd/dot_general | solution.py:61
  216.2 8.2 %fusion.14 = bf16[32,2,14,2048]{3,0,2,1:T(8,128)(2,1)S(1)} fusion(f32[2,32,14,2048]{3,1,2,0:T(8,128)} %fusion, bf16[32,2,14,768]{3,0,2,1:T(8,128)(2,1)S(1)} %get-tuple-element.26, bf16[2,2048,768]{2,1,0:T(8,128)(2,1)} %param.12), kind=kOutput, calls=%fused_computation.21 | convolution fusion | flops 2822242304 | bytes 18677760 | tf_op jit(solution)/shard_map/pecf,edf->pecd/dot_general | solution.py:60
  224.4 5.6 %copy.72 = bf16[32,2,14,2048]{3,1,2,0:T(2,128)(2,1)} copy(bf16[32,2,14,2048]{3,0,2,1:T(8,128)(2,1)S(1)} %fusion.14) | data formatting | bytes 7340032 | tf_op jit(solution)/shard_map/convert_element_type | solution.py:65
  230.0 22.2 %all-to-all-done.1 = bf16[32,2,14,2048]{3,1,2,0:T(2,128)(2,1)} async-done(((bf16[32,2,14,2048]{3,1,2,0:T(2,128)(2,1)}), bf16[32,2,14,2048]{3,1,2,0:T(2,128)(2,1)}, u32[]{:S(2)}, u32[]{:S(2)}) %all-to-all-start.1) | async-done | bytes 3670048 | tf_op jit(solution)/shard_map/all_to_all | solution.py:35
  252.2 7.7 %all-to-all-start.3 = ((bf16[32,2,14,2048]{3,1,2,0:T(2,128)(2,1)}), bf16[32,2,14,2048]{3,1,2,0:T(2,128)(2,1)}, u32[]{:S(2)}, u32[]{:S(2)}) async-start(bf16[32,2,14,2048]{3,1,2,0:T(2,128)(2,1)} %copy.72), calls=%async_computation.3 | async-start | bytes 7340032 | tf_op jit(solution)/shard_map/all_to_all | solution.py:64
  260.1 5.8 %copy.68 = bf16[32,2,14,2048]{3,2,1,0:T(8,128)(2,1)} copy(bf16[32,2,14,2048]{3,1,2,0:T(2,128)(2,1)} %all-to-all-done.1) | data formatting | bytes 7340032 | tf_op jit(solution)/shard_map/all_to_all | solution.py:35
  265.8 6.0 %reshape.59 = bf16[896,2048]{1,0:T(8,128)(2,1)} reshape(bf16[32,2,14,2048]{3,2,1,0:T(8,128)(2,1)} %copy.68) | data formatting | bytes 7340032 | tf_op jit(solution)/shard_map/reshape | solution.py:37
  271.9 5.2 %fusion.13 = (f32[4,128]{1,0:T(4,128)}, bf16[128,2048]{0,1:T(8,128)(2,1)S(1)}) fusion(f32[128,2048]{0,1:T(8,128)S(1)} %copy.74, f32[4,128]{1,0:T(4,128)S(1)} %bitcast.119, s32[128,4]{0,1:T(4,128)S(1)} %multiply_add_fusion, bf16[896,2048]{1,0:T(8,128)(2,1)} %reshape.59), kind=kOutput, calls=%fused_computation.20 | convolution fusion | flops 1883438592 | bytes 5249024 | tf_op jit(solution)/shard_map/srk,sd->krd/dot_general | solution.py:38
  278.1 26.5 %all-to-all-done.3 = bf16[32,2,14,2048]{3,1,2,0:T(2,128)(2,1)} async-done(((bf16[32,2,14,2048]{3,1,2,0:T(2,128)(2,1)}), bf16[32,2,14,2048]{3,1,2,0:T(2,128)(2,1)}, u32[]{:S(2)}, u32[]{:S(2)}) %all-to-all-start.3) | async-done | bytes 3670048 | tf_op jit(solution)/shard_map/all_to_all | solution.py:64
  304.6 6.2 %copy.73 = bf16[32,2,14,2048]{3,2,1,0:T(8,128)(2,1)} copy(bf16[32,2,14,2048]{3,1,2,0:T(2,128)(2,1)} %all-to-all-done.3) | data formatting | bytes 7340032 | tf_op jit(solution)/shard_map/all_to_all | solution.py:64
  310.8 6.1 %reshape.61 = bf16[896,2048]{1,0:T(8,128)(2,1)} reshape(bf16[32,2,14,2048]{3,2,1,0:T(8,128)(2,1)} %copy.73) | data formatting | bytes 7340032 | tf_op jit(solution)/shard_map/reshape | solution.py:68
  316.9 3.6 convolution_convert_fusion.1
  320.6 38.7 %reduce-scatter.6.cloned.1.call-done = bf16[2,512,768]{2,1,0:T(8,128)(2,1)} async-done(((bf16[2,2048,768]{2,1,0:T(8,128)(2,1)}), bf16[2,512,768]{2,1,0:T(8,128)(2,1)}) %reduce-scatter.6.cloned.1.call-update) | async-done | bytes 1572880 | tf_op jit(solution)/shard_map/reduce_scatter | solution.py:79
  (35 shorter events, 7.2 us)
Async XLA Ops:
  7.2 3.3 copy-start
  27.3 10.3 %copy-start.3 = (f32[128,4]{0,1:T(4,128)S(1)}, f32[128,4]{0,1:T(4,128)}, u32[]{:S(2)}) copy-start(f32[128,4]{0,1:T(4,128)} %param.10) | copy-start | bytes 6148
  27.3 10.5 %copy-start.2 = (bf16[128,2048]{1,0:T(8,128)(2,1)S(1)}, bf16[128,2048]{1,0:T(8,128)(2,1)}, u32[]{:S(2)}) copy-start(bf16[128,2048]{1,0:T(8,128)(2,1)} %param.15) | copy-start | bytes 1572868
  27.3 55.2 %all-to-all-start = ((bf16[32,2,14,2048]{3,1,2,0:T(2,128)(2,1)}), bf16[32,2,14,2048]{3,1,2,0:T(2,128)(2,1)}, u32[]{:S(2)}, u32[]{:S(2)}) async-start(bf16[32,2,14,2048]{3,1,2,0:T(2,128)(2,1)} %copy.64), calls=%async_computation | async-start | bytes 7340032 | tf_op jit(solution)/shard_map/all_to_all | solution.py:28
  82.5 52.5 %all-to-all-start.2 = ((bf16[32,2,14,2048]{3,1,2,0:T(2,128)(2,1)}), bf16[32,2,14,2048]{3,1,2,0:T(2,128)(2,1)}, u32[]{:S(2)}, u32[]{:S(2)}) async-start(bf16[32,2,14,2048]{3,1,2,0:T(2,128)(2,1)} %copy.70), calls=%async_computation.2 | async-start | bytes 7340032 | tf_op jit(solution)/shard_map/all_to_all | solution.py:52
  89.8 230.8 %reduce-scatter.8.cloned.1.call-start = ((), (), s32[]{:S(2)}) async-start(), calls=%async_computation.9 | async-start | bytes 7864320 | tf_op jit(solution)/shard_map/reduce_scatter | solution.py:82
  148.4 1.1 copy-start.4
  162.8 157.8 %reduce-scatter.4.cloned.1.call-start = ((), (), s32[]{:S(2)}) async-start(), calls=%async_computation.7 | async-start | bytes 7864320 | tf_op jit(solution)/shard_map/reduce_scatter | solution.py:76
  174.9 184.4 %reduce-scatter.6.cloned.1.call-start = ((), (), s32[]{:S(2)}) async-start(), calls=%async_computation.8 | async-start | bytes 7864320 | tf_op jit(solution)/shard_map/reduce_scatter | solution.py:79
  199.6 52.6 %all-to-all-start.1 = ((bf16[32,2,14,2048]{3,1,2,0:T(2,128)(2,1)}), bf16[32,2,14,2048]{3,1,2,0:T(2,128)(2,1)}, u32[]{:S(2)}, u32[]{:S(2)}) async-start(bf16[32,2,14,2048]{3,1,2,0:T(2,128)(2,1)} %copy.67), calls=%async_computation.1 | async-start | bytes 7340032 | tf_op jit(solution)/shard_map/all_to_all | solution.py:35
  252.2 52.4 %all-to-all-start.3 = ((bf16[32,2,14,2048]{3,1,2,0:T(2,128)(2,1)}), bf16[32,2,14,2048]{3,1,2,0:T(2,128)(2,1)}, u32[]{:S(2)}, u32[]{:S(2)}) async-start(bf16[32,2,14,2048]{3,1,2,0:T(2,128)(2,1)} %copy.72), calls=%async_computation.3 | async-start | bytes 7340032 | tf_op jit(solution)/shard_map/all_to_all | solution.py:64
  310.8 48.4 %copy-start.1 = (bf16[128,2048]{1,0:T(8,128)(2,1)S(1)}, bf16[128,2048]{1,0:T(8,128)(2,1)}, u32[]{:S(2)}) copy-start(bf16[128,2048]{1,0:T(8,128)(2,1)} %param.8) | copy-start | bytes 1572868
Sparse Core Ops, SparseCore 0:
  162.9 62.9 reduce-scatter.7
  228.9 63.6 reduce-scatter.3
  295.6 63.6 reduce-scatter.5
where the time goes:
time: 372 us; the launch traced here: 366 us
  waiting for transfers between devices  138 us (37%)
  matrix products  111 us (30%)
  local copies, waits for them, and re-layouts  66.3 us (18%)
  starting transfers between devices  33.8 us (9%)
  between operations  14.1 us (4%)
    reduce_scatter x1, waiting for transfers between devices, on_device(): lax.psum_scatter(term_up.astype(jnp.bfloat16), 'dp', scatter_dimension=1,...  38.7 us
    all_to_all x1, waiting for transfers between devices, on_device(): lax.all_to_all(send_rows, 'expert', split_axis=0, concat_axis=0, tiled=True)  27.7 us
    all_to_all x1, waiting for transfers between devices, on_device(): lax.all_to_all(d_inputs.astype(jnp.bfloat16), 'expert', split_axis=0, con...  26.5 us
    all_to_all x1, waiting for transfers between devices, on_device(): lax.all_to_all(d_send, 'expert', split_axis=0, concat_axis=0, tiled=True)  22.8 us
    all_to_all x1, waiting for transfers between devices, on_device(): lax.all_to_all(outputs, 'expert', split_axis=0, concat_axis=0, tiled=True)  22.2 us
    reshape x2, local copies, waits for them, and re-layouts, on_device(): d_send = (gate_spot[:, None] * d_spots).astype(jnp.bfloat16).reshape(peer...  13.9 us
    reshape x2, local copies, waits for them, and re-layouts, on_device(): send_rows = send_rows.reshape(peer_count, local_count, capacity, width)  13.8 us
    dot_general x1, matrix products, on_device(): jnp.einsum('pecd,efd->pecf', d_rows, w_down, preferred_element_type=jnp.f...  13.4 us
  transfers between devices with their start and end apart: 7, of which 5 were waited for; matrix products, arithmetic and copies ran while one was open for 36% of the time, Pallas kernels for 0%

commit v1 on v0

v1 whole, which is shorter than its diff:
```python
import functools

import jax
import jax.numpy as jnp
from jax import lax
from jax.experimental import pallas as pl
from jax.experimental.pallas import tpu as pltpu
from jax.sharding import PartitionSpec as P

MESH = pl.DeviceIdType.MESH
F32 = jnp.float32
BF16 = jnp.bfloat16
NT = (((1,), (1,)), ((), ()))
TN = (((0,), (0,)), ((), ()))


def mm(a, b):
    return jnp.dot(a, b, preferred_element_type=F32)


def mm_nt(a, b):
    return lax.dot_general(a, b, NT, preferred_element_type=F32)


def mm_tn(a, b):
    return lax.dot_general(a, b, TN, preferred_element_type=F32)


def kernel(
    n, ring, pos_t, pos, gates_t, gates, tok, dout, wg_h, wu_h, wd_h,
    lo, dt, dg, gg, gu, gd, ret, r2w, r2d,
    send, land, wg, wu, wd, act, hid, pw, pd, r1w, r1d, tw, td,
    f_send, f_recv, b_send, b_recv, w_sem, g_send, g_recv, l_sem, o_sem,
):
    me = lax.axis_index("expert")
    r = lax.axis_index("dp")
    right, left, opp = lax.rem(r + 1, ring), lax.rem(r + 3, ring), lax.rem(r + 2, ring)
    slots, _, pad, width = send.shape[1:]
    rows = n * pad
    ff = wg.shape[1]
    chunk = width // ring
    ft = 256
    tops = gates.shape[1]

    barrier = pltpu.get_barrier_semaphore()

    def greet(i, _):
        pl.semaphore_signal(
            barrier, inc=1, device_id={"expert": lax.rem(me + i, n)}, device_id_type=MESH
        )
        return 0

    lax.fori_loop(1, n, greet, 0)
    for side in (right, left):
        pl.semaphore_signal(barrier, inc=1, device_id={"dp": side}, device_id_type=MESH)

    def weight_copies(s):
        return [
            pltpu.make_async_copy(src.at[s], dst, w_sem.at[j])
            for j, (src, dst) in enumerate(((wg_h, wg), (wu_h, wu), (wd_h, wd)))
        ]

    for copy in weight_copies(0):
        copy.start()

    def fill(s):
        spot = lax.broadcasted_iota(jnp.int32, (rows, pos_t.shape[1]), 0) + s * rows
        picked = jnp.zeros(spot.shape, F32)
        weight = jnp.zeros(spot.shape, F32)
        for k in range(tops):
            hit = pos_t[k : k + 1, :] == spot
            picked = jnp.where(hit, 1.0, picked)
            weight = jnp.where(hit, gates_t[k : k + 1, :], weight)
        picked = picked.astype(BF16)
        weight = jnp.sum(weight, axis=1, keepdims=True)

        def tile(j, _):
            cols = pl.ds(pl.multiple_of(j * chunk, chunk), chunk)
            send[0, s, :, :, cols] = mm(picked, tok[:, cols]).astype(BF16).reshape(n, pad, chunk)
            rows_d = mm(picked, dout[:, cols]) * weight
            send[1, s, :, :, cols] = rows_d.astype(BF16).reshape(n, pad, chunk)
            return 0

        lax.fori_loop(0, width // chunk, tile, 0)

    def exchange(k, s, dst, s_sem, r_sem):
        pltpu.make_async_copy(send.at[k, s, me], dst.at[k, s, me], r_sem.at[k, s]).start()

        def go(i, _):
            peer = lax.rem(me + i, n)
            pltpu.make_async_remote_copy(
                src_ref=send.at[k, s, peer],
                dst_ref=dst.at[k, s, me],
                send_sem=s_sem.at[k, s],
                recv_sem=r_sem.at[k, s],
                device_id={"expert": peer},
                device_id_type=MESH,
            ).start()
            return 0

        lax.fori_loop(1, n, go, 0)

    def wait_recv(k, s, dst, r_sem):
        pltpu.make_async_copy(dst.at[k, s], dst.at[k, s], r_sem.at[k, s]).wait()

    def wait_send(k, s, s_sem):
        part = send.at[k, s, pl.ds(0, n - 1)]
        pltpu.make_async_copy(part, part, s_sem.at[k, s]).wait()

    items = (
        (pd, r1d, r2d, td, gd),
        (pw.at[0], r1w.at[0], r2w.at[0], tw, gg),
        (pw.at[1], r1w.at[1], r2w.at[1], tw, gu),
    )

    def ring_copy(item, s, step, side):
        part, first, second, _, _ = items[item]
        half = part.shape[2] // 2
        low, high = pl.ds(0, half), pl.ds(half, half)
        near = right if side == 0 else left
        if step == 0:
            rows_s = low if side == 0 else high
            src, dst = part.at[s, opp, rows_s], first.at[s, side]
        else:
            rows_s = (high if side == 0 else low) if step == 1 else (low if side == 0 else high)
            src, dst = part.at[s, near, rows_s], second.at[s, side, rows_s]
        return pltpu.make_async_remote_copy(
            src_ref=src,
            dst_ref=dst,
            send_sem=g_send.at[s, item, step, side],
            recv_sem=g_recv.at[s, item, step, side],
            device_id={"dp": near},
            device_id_type=MESH,
        )

    def ring_start(item, s):
        for step in (0, 1):
            for side in (0, 1):
                ring_copy(item, s, step, side).start()

    def add_rows(dst, src, count):
        block = 64

        def go(j, _):
            at = pl.ds(pl.multiple_of(j * block, block), block)
            dst[at, :] = (dst[at, :].astype(F32) + src[at, :].astype(F32)).astype(BF16)
            return 0

        lax.fori_loop(0, count // block, go, 0)

    def ring_middle(item, s):
        part, first, _, _, _ = items[item]
        half = part.shape[2] // 2
        for side in (0, 1):
            near = right if side == 0 else left
            at = pl.ds(0, half) if side == 0 else pl.ds(half, half)
            ring_copy(item, s, 0, side).wait_recv()
            add_rows(part.at[s, near, at], first.at[s, side], half)
            ring_copy(item, s, 2, side).start()

    def ring_end(item, s):
        part, _, second, temp, out = items[item]
        count = part.shape[2]
        for side in (0, 1):
            for step in (1, 2):
                ring_copy(item, s, step, side).wait_recv()
        loads = [
            pltpu.make_async_copy(second.at[s, side], temp.at[side], l_sem.at[side])
            for side in (0, 1)
        ]
        for copy in loads:
            copy.start()
        for copy in loads:
            copy.wait()
        block = 64
        own = part.at[s, r]

        def go(j, _):
            at = pl.ds(pl.multiple_of(j * block, block), block)
            total = own[at, :].astype(F32) + temp[0, at, :].astype(F32) + temp[1, at, :].astype(F32)
            own[at, :] = total.astype(BF16)
            return 0

        lax.fori_loop(0, count // block, go, 0)
        pltpu.make_async_copy(own, out.at[s], o_sem.at[s, item]).start()

    def rows_of(k, s, cols):
        return land[k, s, :, :, cols].reshape(rows, -1)

    def compute(s, _):
        for copy in weight_copies(s):
            copy.wait()
        wait_recv(0, s, land, f_recv)

        def first(j, _):
            cols = pl.ds(pl.multiple_of(j * ft, ft), ft)
            x = rows_of(0, s, slice(None))
            gate = mm(x, wg[:, cols])
            up = mm(x, wu[:, cols])
            sigma = jax.nn.sigmoid(gate)
            silu = gate * sigma
            hid[0, :, cols] = (silu * up).astype(BF16)
            act[0, :, cols] = up * sigma * (1.0 + gate * (1.0 - sigma))
            act[1, :, cols] = silu
            return 0

        lax.fori_loop(0, ff // ft, first, 0)
        wait_send(0, s, f_send)

        def out_tile(j, _):
            cols = pl.ds(pl.multiple_of(j * chunk, chunk), chunk)
            send[0, s, :, :, cols] = mm(hid[0], wd[:, cols]).astype(BF16).reshape(n, pad, chunk)
            return 0

        lax.fori_loop(0, ring, out_tile, 0)
        exchange(0, s, ret, b_send, b_recv)

        wait_recv(1, s, land, f_recv)

        def down_tile(j, _):
            cols = pl.ds(pl.multiple_of(j * chunk, chunk), chunk)
            pd[s, j] = mm_tn(hid[0], rows_of(1, s, cols)).astype(BF16)
            return 0

        lax.fori_loop(0, ring, down_tile, 0)
        ring_start(0, s)

        def back(j, _):
            cols = pl.ds(pl.multiple_of(j * ft, ft), ft)
            d_hid = mm_nt(rows_of(1, s, slice(None)), wd[cols, :])
            hid[1, :, cols] = (d_hid * act[0, :, cols]).astype(BF16)
            hid[2, :, cols] = (d_hid * act[1, :, cols]).astype(BF16)
            return 0

        lax.fori_loop(0, ff // ft, back, 0)
        for item in (0, 1):

            def up_tile(j, _):
                cols = pl.ds(pl.multiple_of(j * chunk, chunk), chunk)
                pw[item, s, j] = mm_tn(rows_of(0, s, cols), hid[1 + item]).astype(BF16)
                return 0

            lax.fori_loop(0, ring, up_tile, 0)
            ring_start(1 + item, s)
        wait_send(1, s, f_send)

        def in_tile(j, _):
            cols = pl.ds(pl.multiple_of(j * chunk, chunk), chunk)
            total = mm_nt(hid[1], wg[cols, :]) + mm_nt(hid[2], wu[cols, :])
            send[1, s, :, :, cols] = total.astype(BF16).reshape(n, pad, chunk)
            return 0

        lax.fori_loop(0, ring, in_tile, 0)
        exchange(1, s, ret, b_send, b_recv)

        @pl.when(s + 1 < slots)
        def _():
            for copy in weight_copies(s + 1):
                copy.start()

        for item in range(3):
            ring_middle(item, s)
        return 0

    fill(0)
    pl.semaphore_wait(barrier, n + 1)
    for k in (0, 1):
        exchange(k, 0, land, f_send, f_recv)
    for s in range(1, slots):
        fill(s)
        for k in (0, 1):
            exchange(k, s, land, f_send, f_recv)
    lax.fori_loop(0, slots, compute, 0)

    spots = slots * rows
    loads = [pltpu.make_async_copy(ret.at[k], land.at[k], l_sem.at[k]) for k in (0, 1)]
    for k in (0, 1):
        for s in range(slots):
            wait_recv(k, s, ret, b_recv)
        loads[k].start()
    spot = lax.broadcasted_iota(jnp.int32, (pos.shape[0], spots), 1)
    hits = [pos[:, k : k + 1] == spot for k in range(tops)]
    hits = [jnp.where(hit, 1.0, 0.0) for hit in hits]
    whole = sum(hits).astype(BF16)
    hits = [hit.astype(BF16) for hit in hits]
    for copy in loads:
        copy.wait()

    def combine(j, sums):
        cols = pl.ds(pl.multiple_of(j * chunk, chunk), chunk)
        outs = land[0, :, :, :, cols].reshape(spots, chunk)
        d_ins = land[1, :, :, :, cols].reshape(spots, chunk)
        d_here = dout[:, cols].astype(F32)
        layer = jnp.zeros(d_here.shape, F32)
        result = []
        for k in range(tops):
            got = mm(hits[k], outs)
            layer = layer + gates[:, k : k + 1] * got
            result.append(sums[k] + jnp.sum(d_here * got, axis=1, keepdims=True))
        lo[:, cols] = layer.astype(BF16)
        dt[:, cols] = mm(whole, d_ins).astype(BF16)
        return tuple(result)

    zero = jnp.zeros((pos.shape[0], 1), F32)
    sums = lax.fori_loop(0, ring, combine, (zero,) * tops)
    for k in range(tops):
        dg[:, k : k + 1] = sums[k]

    for s in range(slots):
        for item in range(3):
            ring_end(item, s)
    for s in range(slots):
        for item in range(3):
            part, _, _, _, out = items[item]
            pltpu.make_async_copy(part.at[s, r], out.at[s], o_sem.at[s, item]).wait()
            for step in range(3):
                for side in (0, 1):
                    ring_copy(item, s, step, side).wait_send()
        for k in (0, 1):
            wait_send(k, s, b_send)


def on_device(n, ring, tokens, expert_ids, gate_weights, slot_of_expert, w_gate, w_up, w_down, d_out):
    slots, width, ff = w_gate.shape
    tok_rows, tops = expert_ids.shape
    experts = slots * n
    capacity = tok_rows * tops * 7 // (4 * experts)
    pad = -(-capacity // 16) * 16
    rows = n * pad
    chunk = width // ring

    wide = jnp.arange(experts, dtype=jnp.int32)
    slot = jnp.sum(jnp.where(expert_ids[:, :, None] == wide, slot_of_expert, 0), axis=2)
    named = slot[:, :, None] == wide
    earlier = jnp.arange(tok_rows)[:, None] > jnp.arange(tok_rows)[None, :]
    before = jnp.dot(
        earlier.astype(BF16), jnp.any(named, axis=1).astype(BF16), preferred_element_type=F32
    )
    rank = jnp.sum(jnp.where(named, before[:, None, :], 0.0), axis=2).astype(jnp.int32)
    pos = (slot % slots) * rows + (slot // slots) * pad + rank

    vmem = pl.BlockSpec(memory_space=pltpu.VMEM)
    hbm = pl.BlockSpec(memory_space=pl.ANY)
    out = pl.pallas_call(
        functools.partial(kernel, n, ring),
        out_shape=[
            jax.ShapeDtypeStruct((tok_rows, width), BF16),
            jax.ShapeDtypeStruct((tok_rows, width), BF16),
            jax.ShapeDtypeStruct((tok_rows, tops), F32),
            jax.ShapeDtypeStruct((slots, chunk, ff), BF16),
            jax.ShapeDtypeStruct((slots, chunk, ff), BF16),
            jax.ShapeDtypeStruct((slots, ff, chunk), BF16),
            jax.ShapeDtypeStruct((2, slots, n, pad, width), BF16),
            jax.ShapeDtypeStruct((2, slots, 2, chunk, ff), BF16),
            jax.ShapeDtypeStruct((slots, 2, ff, chunk), BF16),
        ],
        in_specs=[vmem] * 6 + [hbm] * 3,
        out_specs=[vmem] * 3 + [hbm] * 6,
        scratch_shapes=[
            pltpu.VMEM((2, slots, n, pad, width), BF16),
            pltpu.VMEM((2, slots, n, pad, width), BF16),
            pltpu.VMEM((width, ff), BF16),
            pltpu.VMEM((width, ff), BF16),
            pltpu.VMEM((ff, width), BF16),
            pltpu.VMEM((2, rows, ff), F32),
            pltpu.VMEM((3, rows, ff), BF16),
            pltpu.VMEM((2, slots, ring, chunk, ff), BF16),
            pltpu.VMEM((slots, ring, ff, chunk), BF16),
            pltpu.VMEM((2, slots, 2, chunk // 2, ff), BF16),
            pltpu.VMEM((slots, 2, ff // 2, chunk), BF16),
            pltpu.VMEM((2, chunk, ff), BF16),
            pltpu.VMEM((2, ff, chunk), BF16),
            pltpu.SemaphoreType.DMA((2, slots)),
            pltpu.SemaphoreType.DMA((2, slots)),
            pltpu.SemaphoreType.DMA((2, slots)),
            pltpu.SemaphoreType.DMA((2, slots)),
            pltpu.SemaphoreType.DMA((3,)),
            pltpu.SemaphoreType.DMA((slots, 3, 3, 2)),
            pltpu.SemaphoreType.DMA((slots, 3, 3, 2)),
            pltpu.SemaphoreType.DMA((2,)),
            pltpu.SemaphoreType.DMA((slots, 3)),
        ],
        compiler_params=pltpu.CompilerParams(
            collective_id=0, has_side_effects=True, vmem_limit_bytes=63 * 1024 * 1024
        ),
    )(pos.T, pos, gate_weights.T, gate_weights, tokens, d_out, w_gate, w_up, w_down)
    return tuple(out[:6])


def solution(mesh):
    token = P(("dp", "expert"), None)
    weight = P("expert", None, None)
    return jax.shard_map(
        functools.partial(on_device, mesh.shape["expert"], mesh.shape["dp"]),
        mesh=mesh,
        in_specs=(token, token, token, P(), weight, weight, weight, token),
        out_specs=(
            token, token, token,
            P("expert", "dp", None), P("expert", "dp", None), P("expert", None, "dp"),
        ),
        check_vma=False,
    )
```

time: 372 us -> 257 us (0.69)
  Pallas kernels: 0 us -> 237 us
  waiting for transfers between devices: 138 us -> 0 us
  matrix products: 111 us -> 0.14 us
  local copies, waits for them, and re-layouts: 66.3 us -> 12.1 us
  starting transfers between devices: 33.8 us -> 0 us
  between operations: 14.1 us -> 0.66 us
    pallas_call x0 -> x1, Pallas kernels: none -> 237 us  [on_device(): pl.pallas_call(functools.partial(kernel, n, ring), out_shape=[jax.ShapeDt...]
    dot_general x13 -> x1, matrix products: 111 us -> 0.14 us  [on_device(): jnp.dot(earlier.astype(BF16), jnp.any(named, axis=1).astype(BF16), prefer...]
    all_to_all x4 -> x0, waiting for transfers between devices: 99.3 us -> none  [the longest x1 27.7 us: on_device(): lax.all_to_all(send_rows, 'expert', split_axis=0, concat_axis=0, tiled=True)]
    reshape x6 -> x0, local copies, waits for them, and re-layouts: 39.9 us -> none  [the longest x2 13.9 us: on_device(): d_send = (gate_spot[:, None] * d_spots).astype(jnp.bfloat16).reshape(peer...]
    reduce_scatter x3 -> x0, waiting for transfers between devices: 38.7 us -> none  [the longest x1 38.7 us: on_device(): lax.psum_scatter(term_up.astype(jnp.bfloat16), 'dp', scatter_dimension=1,...]
    all_to_all x4 -> x0, starting transfers between devices: 32.5 us -> none  [the longest x1 10.3 us: on_device(): lax.all_to_all(send_rows, 'expert', split_axis=0, concat_axis=0, tiled=True)]
    all_to_all x2 -> x0, local copies, waits for them, and re-layouts: 11.9 us -> none  [the longest x1 6.17 us: on_device(): lax.all_to_all(d_inputs.astype(jnp.bfloat16), 'expert', split_axis=0, con...]
    convert_element_type x3 -> x1, local copies, waits for them, and re-layouts: 11.5 us -> 0.12 us  [on_device(): jnp.sum(jnp.where(named, before[:, None, :], 0.0), axis=2).astype(jnp.int32)]
  transfers between devices with their start and end apart: 7 -> 0, of which waited for: 5 -> 0; matrix products, arithmetic and copies ran while one was open for 36% -> 0% of each run, Pallas kernels for 0% -> 0%
where the time goes in v1:
time: 257 us; the launch traced here: 252 us
  Pallas kernels  237 us (92%)
  local copies, waits for them, and re-layouts  12.1 us (5%)
    pallas_call x1, Pallas kernels, on_device(): pl.pallas_call(functools.partial(kernel, n, ring), out_shape=[jax.ShapeDt...  237 us
    unnamed x11, local copies, waits for them, and re-layouts  11.8 us

profile of v1, /device:TPU:1, one launch (start us, length us, event | category | flops | bytes accessed | tf_op | source)
XLA Modules:
  0.0 252.5 jit_solution(6046483037435926768)
XLA Ops:
  0.6 0.8 select_reduce_fusion.1
  1.4 0.1 fusion.7
  1.6 0.6 fusion.12.pos_t
  2.2 0.1 copy.32
  2.4 0.1 copy.28
  2.5 0.7 fusion.3.pos
  3.2 1.4 copy.33.gates
  4.6 237.4 %shard_map.127 = (bf16[128,2048]{1,0:T(8,128)(2,1)}, bf16[128,2048]{1,0:T(8,128)(2,1)}, f32[128,4]{1,0:T(8,128)}, bf16[2,512,768]{2,1,0:T(8,128)(2,1)}, bf16[2,5...) custom-call(s32[4,128]{1,0:T(4,128)} %fusion.12.pos_t, ...), custom_call_target="tpu_custom_call" | custom-call | tf_op jit(solution)/shard_map/pallas_call | solution.py:344
  242.0 0.0 copy-start.1
  242.0 1.6 copy.34
  243.7 1.9 copy.40
  245.5 1.9 copy.41
  247.4 0.0 copy-start
  247.4 2.8 %copy.42 = bf16[2,512,768]{2,1,0:T(8,128)(2,1)} copy(bf16[2,512,768]{2,1,0:T(8,128)(2,1)} %get-tuple-element.45) | data formatting | bytes 3145728
  250.2 0.0 copy-done.1
  250.2 1.1 copy.43
  251.3 0.0 copy-done
  251.3 1.1 copy.44
  (3 shorter events, 0.1 us)
Async XLA Ops:
  242.0 8.2 %copy-start.1 = (bf16[2,512,768]{2,1,0:T(8,128)(2,1)S(1)}, bf16[2,512,768]{2,1,0:T(8,128)(2,1)}, u32[]{:S(2)}) copy-start(bf16[2,512,768]{2,1,0:T(8,128)(2,1)} %get-tuple-element.46) | copy-start | bytes 4718596
  247.4 3.9 %copy-start = (bf16[2,768,512]{2,1,0:T(8,128)(2,1)S(1)}, bf16[2,768,512]{2,1,0:T(8,128)(2,1)}, u32[]{:S(2)}) copy-start(bf16[2,768,512]{2,1,0:T(8,128)(2,1)} %get-tuple-element.47) | copy-start | bytes 4718596

commit v2 on v1

--- a/solution.py
+++ b/solution.py
@@ -8,6 +8,7 @@
 from jax.sharding import PartitionSpec as P
 
 MESH = pl.DeviceIdType.MESH
+STRIDE = 3
 F32 = jnp.float32
 BF16 = jnp.bfloat16
 NT = (((1,), (1,)), ((), ()))
@@ -83,19 +84,24 @@
 
         lax.fori_loop(0, width // chunk, tile, 0)
 
+    def keep(k, s, dst, r_sem):
+        pltpu.make_async_copy(send.at[k, s, me], dst.at[k, s, me], r_sem.at[k, s]).start()
+
+    def row_copy(k, s, peer, dst, s_sem, r_sem):
+        return pltpu.make_async_remote_copy(
+            src_ref=send.at[k, s, peer],
+            dst_ref=dst.at[k, s, me],
+            send_sem=s_sem.at[k, s],
+            recv_sem=r_sem.at[k, s],
+            device_id={"expert": peer},
+            device_id_type=MESH,
+        )
+
     def exchange(k, s, dst, s_sem, r_sem):
-        pltpu.make_async_copy(send.at[k, s, me], dst.at[k, s, me], r_sem.at[k, s]).start()
+        keep(k, s, dst, r_sem)
 
         def go(i, _):
-            peer = lax.rem(me + i, n)
-            pltpu.make_async_remote_copy(
-                src_ref=send.at[k, s, peer],
-                dst_ref=dst.at[k, s, me],
-                send_sem=s_sem.at[k, s],
-                recv_sem=r_sem.at[k, s],
-                device_id={"expert": peer},
-                device_id_type=MESH,
-            ).start()
+            row_copy(k, s, lax.rem(me + 5 * i, n), dst, s_sem, r_sem).start()
             return 0
 
         lax.fori_loop(1, n, go, 0)
@@ -262,15 +268,35 @@
             ring_middle(item, s)
         return 0
 
+    def dispatch(s):
+        for k in (0, 1):
+            keep(k, s, land, f_recv)
+        for core in (0, 1):
+            for k in (0, 1):
+
+                def go(i, _):
+                    chip = lax.rem(me // 2 + STRIDE * i, n // 2)
+                    peer = chip * 2 + core
+
+                    @pl.when(peer != me)
+                    def _():
+                        row_copy(k, s, peer, land, f_send, f_recv).start()
+
+                    return 0
+
+                lax.fori_loop(0, n // 2, go, 0)
+
     fill(0)
     pl.semaphore_wait(barrier, n + 1)
-    for k in (0, 1):
-        exchange(k, 0, land, f_send, f_recv)
+    dispatch(0)
     for s in range(1, slots):
         fill(s)
-        for k in (0, 1):
-            exchange(k, s, land, f_send, f_recv)
+        dispatch(s)
     lax.fori_loop(0, slots, compute, 0)
+
+    for s in range(slots - 1):
+        for item in range(3):
+            ring_end(item, s)
 
     spots = slots * rows
     loads = [pltpu.make_async_copy(ret.at[k], land.at[k], l_sem.at[k]) for k in (0, 1)]
@@ -306,9 +332,8 @@
     for k in range(tops):
         dg[:, k : k + 1] = sums[k]
 
-    for s in range(slots):
-        for item in range(3):
-            ring_end(item, s)
+    for item in range(3):
+        ring_end(item, slots - 1)
     for s in range(slots):
         for item in range(3):
             part, _, _, _, out = items[item]

time: 257 us -> 225 us (0.88); the launches traced: 252 us -> 225 us
  Pallas kernels: 237 us -> 209 us
    pallas_call x1, Pallas kernels: 237 us -> 209 us  [on_device(): pl.pallas_call(functools.partial(kernel, n, ring), out_shape=[jax.ShapeDt...]
where the time goes in v2:
time: 225 us
  Pallas kernels  209 us (93%)
  local copies, waits for them, and re-layouts  12.1 us (5%)
    pallas_call x1, Pallas kernels, on_device(): pl.pallas_call(functools.partial(kernel, n, ring), out_shape=[jax.ShapeDt...  209 us
    unnamed x11, local copies, waits for them, and re-layouts  11.8 us

profile of v2, /device:TPU:1, one launch (start us, length us, event | category | flops | bytes accessed | tf_op | source)
XLA Modules:
  0.0 224.5 jit_solution(1802796333311305798)
XLA Ops:
  0.6 0.8 select_reduce_fusion.1
  1.4 0.1 fusion.7
  1.6 0.6 fusion.12.pos_t
  2.2 0.1 copy.32
  2.4 0.1 copy.28
  2.5 0.7 fusion.3.pos
  3.2 1.4 copy.33.gates
  4.6 209.5 %shard_map.127 = (bf16[128,2048]{1,0:T(8,128)(2,1)}, bf16[128,2048]{1,0:T(8,128)(2,1)}, f32[128,4]{1,0:T(8,128)}, bf16[2,512,768]{2,1,0:T(8,128)(2,1)}, bf16[2,5...) custom-call(s32[4,128]{1,0:T(4,128)} %fusion.12.pos_t, ...), custom_call_target="tpu_custom_call" | custom-call | tf_op jit(solution)/shard_map/pallas_call | solution.py:369
  214.1 0.0 copy-start.1
  214.1 1.6 copy.34
  215.7 1.9 copy.40
  217.6 1.9 copy.41
  219.5 0.0 copy-start
  219.5 2.8 %copy.42 = bf16[2,512,768]{2,1,0:T(8,128)(2,1)} copy(bf16[2,512,768]{2,1,0:T(8,128)(2,1)} %get-tuple-element.45) | data formatting | bytes 3145728
  222.2 0.0 copy-done.1
  222.2 1.1 copy.43
  223.4 0.0 copy-done
  223.4 1.1 copy.44
  (3 shorter events, 0.1 us)
Async XLA Ops:
  214.1 8.2 %copy-start.1 = (bf16[2,512,768]{2,1,0:T(8,128)(2,1)S(1)}, bf16[2,512,768]{2,1,0:T(8,128)(2,1)}, u32[]{:S(2)}) copy-start(bf16[2,512,768]{2,1,0:T(8,128)(2,1)} %get-tuple-element.46) | copy-start | bytes 4718596
  219.5 3.9 %copy-start = (bf16[2,768,512]{2,1,0:T(8,128)(2,1)S(1)}, bf16[2,768,512]{2,1,0:T(8,128)(2,1)}, u32[]{:S(2)}) copy-start(bf16[2,768,512]{2,1,0:T(8,128)(2,1)} %get-tuple-element.47) | copy-start | bytes 4718596

commit v3 on v2

--- a/solution.py
+++ b/solution.py
@@ -28,9 +28,9 @@
 
 
 def kernel(
-    n, ring, pos_t, pos, gates_t, gates, tok, dout, wg_h, wu_h, wd_h,
-    lo, dt, dg, gg, gu, gd, ret, r2w, r2d,
-    send, land, wg, wu, wd, act, hid, pw, pd, r1w, r1d, tw, td,
+    n, ring, gates_pos, tok, dout, wg_h, wu_h, wd_h,
+    lo, dt, dg, own_w, own_d, ret, r2w, r2d,
+    send, land, wg, wu, wd, act, hid, pw, pd, r1w, r1d,
     f_send, f_recv, b_send, b_recv, w_sem, g_send, g_recv, l_sem, o_sem,
 ):
     me = lax.axis_index("expert")
@@ -41,7 +41,8 @@
     ff = wg.shape[1]
     chunk = width // ring
     ft = 256
-    tops = gates.shape[1]
+    tops = gates_pos.shape[0] // 2
+    tok_rows = tok.shape[0]
 
     barrier = pltpu.get_barrier_semaphore()
 
@@ -65,13 +66,13 @@
         copy.start()
 
     def fill(s):
-        spot = lax.broadcasted_iota(jnp.int32, (rows, pos_t.shape[1]), 0) + s * rows
+        spot = lax.broadcasted_iota(jnp.int32, (rows, tok_rows), 0) + s * rows
         picked = jnp.zeros(spot.shape, F32)
         weight = jnp.zeros(spot.shape, F32)
         for k in range(tops):
-            hit = pos_t[k : k + 1, :] == spot
+            hit = gates_pos[tops + k : tops + k + 1, :].astype(jnp.int32) == spot
             picked = jnp.where(hit, 1.0, picked)
-            weight = jnp.where(hit, gates_t[k : k + 1, :], weight)
+            weight = jnp.where(hit, gates_pos[k : k + 1, :], weight)
         picked = picked.astype(BF16)
         weight = jnp.sum(weight, axis=1, keepdims=True)
 
@@ -114,13 +115,13 @@
         pltpu.make_async_copy(part, part, s_sem.at[k, s]).wait()
 
     items = (
-        (pd, r1d, r2d, td, gd),
-        (pw.at[0], r1w.at[0], r2w.at[0], tw, gg),
-        (pw.at[1], r1w.at[1], r2w.at[1], tw, gu),
+        (pd, r1d, r2d, own_d),
+        (pw.at[0], r1w.at[0], r2w.at[0], own_w.at[0]),
+        (pw.at[1], r1w.at[1], r2w.at[1], own_w.at[1]),
     )
 
     def ring_copy(item, s, step, side):
-        part, first, second, _, _ = items[item]
+        part, first, second, _ = items[item]
         half = part.shape[2] // 2
         low, high = pl.ds(0, half), pl.ds(half, half)
         near = right if side == 0 else left
@@ -129,7 +130,7 @@
             src, dst = part.at[s, opp, rows_s], first.at[s, side]
         else:
             rows_s = (high if side == 0 else low) if step == 1 else (low if side == 0 else high)
-            src, dst = part.at[s, near, rows_s], second.at[s, side, rows_s]
+            src, dst = part.at[s, near, rows_s], second.at[side, s, rows_s]
         return pltpu.make_async_remote_copy(
             src_ref=src,
             dst_ref=dst,
@@ -155,7 +156,7 @@
         lax.fori_loop(0, count // block, go, 0)
 
     def ring_middle(item, s):
-        part, first, _, _, _ = items[item]
+        part, first, _, _ = items[item]
         half = part.shape[2] // 2
         for side in (0, 1):
             near = right if side == 0 else left
@@ -164,31 +165,9 @@
             add_rows(part.at[s, near, at], first.at[s, side], half)
             ring_copy(item, s, 2, side).start()
 
-    def ring_end(item, s):
-        part, _, second, temp, out = items[item]
-        count = part.shape[2]
-        for side in (0, 1):
-            for step in (1, 2):
-                ring_copy(item, s, step, side).wait_recv()
-        loads = [
-            pltpu.make_async_copy(second.at[s, side], temp.at[side], l_sem.at[side])
-            for side in (0, 1)
-        ]
-        for copy in loads:
-            copy.start()
-        for copy in loads:
-            copy.wait()
-        block = 64
-        own = part.at[s, r]
-
-        def go(j, _):
-            at = pl.ds(pl.multiple_of(j * block, block), block)
-            total = own[at, :].astype(F32) + temp[0, at, :].astype(F32) + temp[1, at, :].astype(F32)
-            own[at, :] = total.astype(BF16)
-            return 0
-
-        lax.fori_loop(0, count // block, go, 0)
-        pltpu.make_async_copy(own, out.at[s], o_sem.at[s, item]).start()
+    def own_copy(item, s):
+        part, _, _, own = items[item]
+        return pltpu.make_async_copy(part.at[s, r], own.at[s], o_sem.at[s, item])
 
     def rows_of(k, s, cols):
         return land[k, s, :, :, cols].reshape(rows, -1)
@@ -224,12 +203,21 @@
         wait_recv(1, s, land, f_recv)
 
         def down_tile(j, _):
-            cols = pl.ds(pl.multiple_of(j * chunk, chunk), chunk)
-            pd[s, j] = mm_tn(hid[0], rows_of(1, s, cols)).astype(BF16)
+            at = lax.rem(opp + j, ring)
+            cols = pl.ds(pl.multiple_of(at * chunk, chunk), chunk)
+            pd[s, at] = mm_tn(hid[0], rows_of(1, s, cols)).astype(BF16)
+
+            @pl.when(j == 0)
+            def _():
+                for side in (0, 1):
+                    ring_copy(0, s, 0, side).start()
+
             return 0
 
         lax.fori_loop(0, ring, down_tile, 0)
-        ring_start(0, s)
+        for side in (0, 1):
+            ring_copy(0, s, 1, side).start()
+        own_copy(0, s).start()
 
         def back(j, _):
             cols = pl.ds(pl.multiple_of(j * ft, ft), ft)
@@ -248,6 +236,7 @@
 
             lax.fori_loop(0, ring, up_tile, 0)
             ring_start(1 + item, s)
+            own_copy(1 + item, s).start()
         wait_send(1, s, f_send)
 
         def in_tile(j, _):
@@ -294,52 +283,63 @@
         dispatch(s)
     lax.fori_loop(0, slots, compute, 0)
 
-    for s in range(slots - 1):
-        for item in range(3):
-            ring_end(item, s)
-
     spots = slots * rows
-    loads = [pltpu.make_async_copy(ret.at[k], land.at[k], l_sem.at[k]) for k in (0, 1)]
-    for k in (0, 1):
-        for s in range(slots):
-            wait_recv(k, s, ret, b_recv)
-        loads[k].start()
-    spot = lax.broadcasted_iota(jnp.int32, (pos.shape[0], spots), 1)
-    hits = [pos[:, k : k + 1] == spot for k in range(tops)]
+    spot = lax.broadcasted_iota(jnp.int32, (tok_rows, spots), 1)
+    columns = gates_pos[...].T
+    hits = [columns[:, tops + k : tops + k + 1].astype(jnp.int32) == spot for k in range(tops)]
     hits = [jnp.where(hit, 1.0, 0.0) for hit in hits]
     whole = sum(hits).astype(BF16)
     hits = [hit.astype(BF16) for hit in hits]
-    for copy in loads:
-        copy.wait()
+
+    def fetch(k):
+        loads = [
+            pltpu.make_async_copy(ret.at[k, s], land.at[k, s], l_sem.at[k, s]) for s in range(slots)
+        ]
+        for s in range(slots):
+            wait_recv(k, s, ret, b_recv)
+            loads[s].start()
+        for s in range(slots):
+            loads[s].wait()
+
+    fetch(0)
 
     def combine(j, sums):
         cols = pl.ds(pl.multiple_of(j * chunk, chunk), chunk)
         outs = land[0, :, :, :, cols].reshape(spots, chunk)
-        d_ins = land[1, :, :, :, cols].reshape(spots, chunk)
         d_here = dout[:, cols].astype(F32)
         layer = jnp.zeros(d_here.shape, F32)
         result = []
         for k in range(tops):
             got = mm(hits[k], outs)
-            layer = layer + gates[:, k : k + 1] * got
+            layer = layer + columns[:, k : k + 1] * got
             result.append(sums[k] + jnp.sum(d_here * got, axis=1, keepdims=True))
         lo[:, cols] = layer.astype(BF16)
-        dt[:, cols] = mm(whole, d_ins).astype(BF16)
         return tuple(result)
 
-    zero = jnp.zeros((pos.shape[0], 1), F32)
+    zero = jnp.zeros((tok_rows, 1), F32)
     sums = lax.fori_loop(0, ring, combine, (zero,) * tops)
+    lane = lax.broadcasted_iota(jnp.int32, (tok_rows, 128), 1)
+    table = jnp.zeros(lane.shape, F32)
     for k in range(tops):
-        dg[:, k : k + 1] = sums[k]
-
-    for item in range(3):
-        ring_end(item, slots - 1)
+        table = jnp.where(lane == k, sums[k], table)
+    dg[...] = table.T[:tops]
+
+    fetch(1)
+
+    def combine_in(j, _):
+        cols = pl.ds(pl.multiple_of(j * chunk, chunk), chunk)
+        dt[:, cols] = mm(whole, land[1, :, :, :, cols].reshape(spots, chunk)).astype(BF16)
+        return 0
+
+    lax.fori_loop(0, ring, combine_in, 0)
+
     for s in range(slots):
         for item in range(3):
-            part, _, _, _, out = items[item]
-            pltpu.make_async_copy(part.at[s, r], out.at[s], o_sem.at[s, item]).wait()
-            for step in range(3):
-                for side in (0, 1):
+            own_copy(item, s).wait()
+            for side in (0, 1):
+                for step in (1, 2):
+                    ring_copy(item, s, step, side).wait_recv()
+                for step in range(3):
                     ring_copy(item, s, step, side).wait_send()
         for k in (0, 1):
             wait_send(k, s, b_send)
@@ -366,21 +366,21 @@
 
     vmem = pl.BlockSpec(memory_space=pltpu.VMEM)
     hbm = pl.BlockSpec(memory_space=pl.ANY)
+    gates_pos = jnp.concatenate([gate_weights.T, pos.T.astype(F32)], axis=0)
     out = pl.pallas_call(
         functools.partial(kernel, n, ring),
         out_shape=[
             jax.ShapeDtypeStruct((tok_rows, width), BF16),
             jax.ShapeDtypeStruct((tok_rows, width), BF16),
-            jax.ShapeDtypeStruct((tok_rows, tops), F32),
-            jax.ShapeDtypeStruct((slots, chunk, ff), BF16),
-            jax.ShapeDtypeStruct((slots, chunk, ff), BF16),
+            jax.ShapeDtypeStruct((tops, tok_rows), F32),
+            jax.ShapeDtypeStruct((2, slots, chunk, ff), BF16),
             jax.ShapeDtypeStruct((slots, ff, chunk), BF16),
             jax.ShapeDtypeStruct((2, slots, n, pad, width), BF16),
-            jax.ShapeDtypeStruct((2, slots, 2, chunk, ff), BF16),
-            jax.ShapeDtypeStruct((slots, 2, ff, chunk), BF16),
+            jax.ShapeDtypeStruct((2, 2, slots, chunk, ff), BF16),
+            jax.ShapeDtypeStruct((2, slots, ff, chunk), BF16),
         ],
-        in_specs=[vmem] * 6 + [hbm] * 3,
-        out_specs=[vmem] * 3 + [hbm] * 6,
+        in_specs=[vmem] * 3 + [hbm] * 3,
+        out_specs=[vmem] * 3 + [hbm] * 5,
         scratch_shapes=[
             pltpu.VMEM((2, slots, n, pad, width), BF16),
             pltpu.VMEM((2, slots, n, pad, width), BF16),
@@ -393,8 +393,6 @@
             pltpu.VMEM((slots, ring, ff, chunk), BF16),
             pltpu.VMEM((2, slots, 2, chunk // 2, ff), BF16),
             pltpu.VMEM((slots, 2, ff // 2, chunk), BF16),
-            pltpu.VMEM((2, chunk, ff), BF16),
-            pltpu.VMEM((2, ff, chunk), BF16),
             pltpu.SemaphoreType.DMA((2, slots)),
             pltpu.SemaphoreType.DMA((2, slots)),
             pltpu.SemaphoreType.DMA((2, slots)),
@@ -402,14 +400,22 @@
             pltpu.SemaphoreType.DMA((3,)),
             pltpu.SemaphoreType.DMA((slots, 3, 3, 2)),
             pltpu.SemaphoreType.DMA((slots, 3, 3, 2)),
-            pltpu.SemaphoreType.DMA((2,)),
+            pltpu.SemaphoreType.DMA((2, slots)),
             pltpu.SemaphoreType.DMA((slots, 3)),
         ],
         compiler_params=pltpu.CompilerParams(
             collective_id=0, has_side_effects=True, vmem_limit_bytes=63 * 1024 * 1024
         ),
-    )(pos.T, pos, gate_weights.T, gate_weights, tokens, d_out, w_gate, w_up, w_down)
-    return tuple(out[:6])
+    )(gates_pos, tokens, d_out, w_gate, w_up, w_down)
+    layer_out, d_tokens, d_gates, own_w, own_d, _, got_w, got_d = out
+
+    def total(own, got):
+        return (own.astype(F32) + got[0].astype(F32) + got[1].astype(F32)).astype(BF16)
+
+    return (
+        layer_out, d_tokens, d_gates.T,
+        total(own_w[0], got_w[0]), total(own_w[1], got_w[1]), total(own_d, got_d),
+    )
 
 
 def solution(mesh):

time: 225 us -> 219 us (0.973)
  local copies, waits for them, and re-layouts: 12.1 us -> 2.18 us
  other arithmetic: 2.16 us -> 10.3 us
  Pallas kernels: 209 us -> 205 us
    unnamed x11, local copies, waits for them, and re-layouts: 11.8 us -> 2.18 us
    convert_element_type x1 -> x3, other arithmetic: 0.01 us -> 8.2 us  [the longest x2 8.18 us: total(): (own.astype(F32) + got[0].astype(F32) + got[1].astype(F32)).astype(BF16)]
    pallas_call x1, Pallas kernels: 209 us -> 205 us  [on_device(): pl.pallas_call(functools.partial(kernel, n, ring), out_shape=[jax.ShapeDt...]
where the time goes in v3:
time: 219 us; the launch traced here: 218 us
  Pallas kernels  205 us (94%)
  other arithmetic  10.3 us (5%)
    pallas_call x1, Pallas kernels, on_device(): pl.pallas_call(functools.partial(kernel, n, ring), out_shape=[jax.ShapeDt...  205 us
    convert_element_type x2, other arithmetic, total(): (own.astype(F32) + got[0].astype(F32) + got[1].astype(F32)).astype(BF16)  8.18 us

profile of v3, /device:TPU:1, one launch (start us, length us, event | category | flops | bytes accessed | tf_op | source)
XLA Modules:
  0.0 218.3 jit_solution(3359693821376311979)
XLA Ops:
  0.6 0.8 select_reduce_fusion.1
  1.4 0.1 fusion.4
  1.7 1.3 pad_maximum_fusion.gates_pos
  2.9 205.0 %shard_map.127 = (bf16[128,2048]{1,0:T(8,128)(2,1)}, bf16[128,2048]{1,0:T(8,128)(2,1)}, f32[4,128]{1,0:T(4,128)}, bf16[2,2,512,768]{3,2,1,0:T(8,128)(2,1)}, bf16...) custom-call(f32[8,128]{1,0:T(8,128)} %pad_maximum_fusion.gates_pos, ...), custom_call_target="tpu_custom_call" | custom-call | tf_op jit(solution)/shard_map/pallas_call | solution.py:370
  207.9 0.0 copy-start
  207.9 4.3 %fusion = bf16[2,768,512]{2,1,0:T(8,128)(2,1)} fusion(bf16[2,768,512]{2,1,0:T(8,128)(2,1)} %get-tuple-element.18, bf16[2,2,768,512]{3,2,1,0:T(8,128)(2,1)} %get-tuple-element.19), kind=kLoop, calls=%fused_computation.1 | loop fusion | flops 4718592 | bytes 6291456 | tf_op jit(solution)/shard_map/convert_element_type | solution.py:413
  212.3 0.0 copy-done
  212.3 0.0 copy-start.2
  212.3 0.0 copy-start.1
  212.3 0.0 copy-start.3
  212.3 3.9 %fusion.1 = (bf16[2,512,768]{2,1,0:T(8,128)(2,1)}, bf16[2,512,768]{2,1,0:T(8,128)(2,1)}) fusion(bf16[2,2,2,512,768]{4,3,2,1,0:T(8,128)(2,1)S(1)} %copy-done, bf16[2,2,512,768]{3,2,1,0:T(8,128)(2,1)} %get-tuple-element.16), kind=kLoop, calls=%fused_computation.4 | loop fusion | flops 9437184 | bytes 12582912 | tf_op jit(solution)/shard_map/convert_element_type | solution.py:413
  216.1 0.0 copy-done.2
  216.1 0.8 copy.20
  216.9 0.0 copy-done.1
  216.9 0.8 copy.21
  217.7 0.0 copy-done.3
  217.7 0.6 copy.22
  (3 shorter events, 0.1 us)
Async XLA Ops:
  207.9 4.3 %copy-start = (bf16[2,2,2,512,768]{4,3,2,1,0:T(8,128)(2,1)S(1)}, bf16[2,2,2,512,768]{4,3,2,1,0:T(8,128)(2,1)}, u32[]{:S(2)}) copy-start(bf16[2,2,2,512,768]{4,3,2,1,0:T(8,128)(2,1)} %get-tuple-element.17) | copy-start | bytes 18874372
  212.3 3.9 %copy-start.2 = (bf16[128,2048]{1,0:T(8,128)(2,1)S(1)}, bf16[128,2048]{1,0:T(8,128)(2,1)}, u32[]{:S(2)}) copy-start(bf16[128,2048]{1,0:T(8,128)(2,1)} %get-tuple-element.28) | copy-start | bytes 1572868
  212.3 4.7 %copy-start.1 = (bf16[128,2048]{1,0:T(8,128)(2,1)S(1)}, bf16[128,2048]{1,0:T(8,128)(2,1)}, u32[]{:S(2)}) copy-start(bf16[128,2048]{1,0:T(8,128)(2,1)} %get-tuple-element.29) | copy-start | bytes 1572868
  212.3 5.5 %copy-start.3 = (f32[4,128]{1,0:T(4,128)S(1)}, f32[4,128]{1,0:T(4,128)}, u32[]{:S(2)}) copy-start(f32[4,128]{1,0:T(4,128)} %get-tuple-element.15) | copy-start | bytes 6148

commit v4 on v3

--- a/solution.py
+++ b/solution.py
@@ -9,6 +9,9 @@
 
 MESH = pl.DeviceIdType.MESH
 STRIDE = 3
+FORWARD_AT = (1, 1, 1, 1)
+RETURN_AT = (1, 1, 2, 3)
+LAST_AT = (0, 0, 0, 0)
 F32 = jnp.float32
 BF16 = jnp.bfloat16
 NT = (((1,), (1,)), ((), ()))
@@ -30,8 +33,8 @@
 def kernel(
     n, ring, gates_pos, tok, dout, wg_h, wu_h, wd_h,
     lo, dt, dg, own_w, own_d, ret, r2w, r2d,
-    send, land, wg, wu, wd, act, hid, pw, pd, r1w, r1d,
-    f_send, f_recv, b_send, b_recv, w_sem, g_send, g_recv, l_sem, o_sem,
+    send, land, wg, wu, wd, act, hid, pw, pd, r1w, r1d, tw, td,
+    f_send, f_recv, b_send, b_recv, w_sem, g_send, g_recv, l_sem, o_sem, t_sem,
 ):
     me = lax.axis_index("expert")
     r = lax.axis_index("dp")
@@ -98,14 +101,39 @@
             device_id_type=MESH,
         )
 
-    def exchange(k, s, dst, s_sem, r_sem):
-        keep(k, s, dst, r_sem)
-
+    def send_part(k, s, core, dst, s_sem, r_sem):
         def go(i, _):
-            row_copy(k, s, lax.rem(me + 5 * i, n), dst, s_sem, r_sem).start()
-            return 0
-
-        lax.fori_loop(1, n, go, 0)
+            chip = lax.rem(me // 2 + STRIDE * i, n // 2)
+            peer = chip * 2 + core
+
+            @pl.when(peer != me)
+            def _():
+                row_copy(k, s, peer, dst, s_sem, r_sem).start()
+
+            return 0
+
+        if core == 0:
+            keep(k, s, dst, r_sem)
+        lax.fori_loop(0, n // 2, go, 0)
+
+    def forward_part(q, s):
+        send_part(q % 2, s, q // 2, land, f_send, f_recv)
+
+    def return_part(q, s):
+        send_part(q // 2, s, q % 2, ret, b_send, b_recv)
+
+    def next_parts(point, s):
+        @pl.when(s + 1 < slots)
+        def _():
+            for q in range(4):
+                if FORWARD_AT[q] == point:
+                    forward_part(q, s + 1)
+
+        @pl.when(s > 0)
+        def _():
+            for q in range(4):
+                if RETURN_AT[q] == point:
+                    return_part(q, s - 1)
 
     def wait_recv(k, s, dst, r_sem):
         pltpu.make_async_copy(dst.at[k, s], dst.at[k, s], r_sem.at[k, s]).wait()
@@ -115,13 +143,13 @@
         pltpu.make_async_copy(part, part, s_sem.at[k, s]).wait()
 
     items = (
-        (pd, r1d, r2d, own_d),
-        (pw.at[0], r1w.at[0], r2w.at[0], own_w.at[0]),
-        (pw.at[1], r1w.at[1], r2w.at[1], own_w.at[1]),
+        (pd, r1d, r2d, own_d, td),
+        (pw.at[0], r1w.at[0], r2w.at[0], own_w.at[0], tw),
+        (pw.at[1], r1w.at[1], r2w.at[1], own_w.at[1], tw),
     )
 
     def ring_copy(item, s, step, side):
-        part, first, second, _ = items[item]
+        part, first, second, _, _ = items[item]
         half = part.shape[2] // 2
         low, high = pl.ds(0, half), pl.ds(half, half)
         near = right if side == 0 else left
@@ -156,7 +184,7 @@
         lax.fori_loop(0, count // block, go, 0)
 
     def ring_middle(item, s):
-        part, first, _, _ = items[item]
+        part, first, _, _, _ = items[item]
         half = part.shape[2] // 2
         for side in (0, 1):
             near = right if side == 0 else left
@@ -166,8 +194,32 @@
             ring_copy(item, s, 2, side).start()
 
     def own_copy(item, s):
-        part, _, _, own = items[item]
+        part, _, _, own, _ = items[item]
         return pltpu.make_async_copy(part.at[s, r], own.at[s], o_sem.at[s, item])
+
+    def ring_end(item, s):
+        part, _, second, _, temp = items[item]
+        loads = [
+            pltpu.make_async_copy(second.at[side, s], temp.at[side], t_sem.at[side])
+            for side in (0, 1)
+        ]
+        for side in (0, 1):
+            for step in (1, 2):
+                ring_copy(item, s, step, side).wait_recv()
+            loads[side].start()
+        for copy in loads:
+            copy.wait()
+        block = 64
+        total = part.at[s, r]
+
+        def go(j, _):
+            at = pl.ds(pl.multiple_of(j * block, block), block)
+            both = temp[0, at, :].astype(F32) + temp[1, at, :].astype(F32)
+            total[at, :] = (total[at, :].astype(F32) + both).astype(BF16)
+            return 0
+
+        lax.fori_loop(0, part.shape[2] // block, go, 0)
+        own_copy(item, s).start()
 
     def rows_of(k, s, cols):
         return land[k, s, :, :, cols].reshape(rows, -1)
@@ -198,8 +250,7 @@
             return 0
 
         lax.fori_loop(0, ring, out_tile, 0)
-        exchange(0, s, ret, b_send, b_recv)
-
+        next_parts(0, s)
         wait_recv(1, s, land, f_recv)
 
         def down_tile(j, _):
@@ -217,7 +268,11 @@
         lax.fori_loop(0, ring, down_tile, 0)
         for side in (0, 1):
             ring_copy(0, s, 1, side).start()
-        own_copy(0, s).start()
+        @pl.when(s == slots - 1)
+        def _():
+            own_copy(0, s).start()
+
+        next_parts(1, s)
 
         def back(j, _):
             cols = pl.ds(pl.multiple_of(j * ft, ft), ft)
@@ -236,7 +291,12 @@
 
             lax.fori_loop(0, ring, up_tile, 0)
             ring_start(1 + item, s)
-            own_copy(1 + item, s).start()
+
+            @pl.when(s == slots - 1)
+            def _():
+                own_copy(1 + item, s).start()
+
+            next_parts(2 + item, s)
         wait_send(1, s, f_send)
 
         def in_tile(j, _):
@@ -246,41 +306,29 @@
             return 0
 
         lax.fori_loop(0, ring, in_tile, 0)
-        exchange(1, s, ret, b_send, b_recv)
-
         @pl.when(s + 1 < slots)
         def _():
             for copy in weight_copies(s + 1):
                 copy.start()
 
-        for item in range(3):
-            ring_middle(item, s)
+        for q in range(4):
+
+            @pl.when(s == slots - 1)
+            def _():
+                for part in range(4):
+                    if LAST_AT[part] == q:
+                        return_part(part, s)
+
+            if q < 3:
+                ring_middle(q, s)
         return 0
-
-    def dispatch(s):
-        for k in (0, 1):
-            keep(k, s, land, f_recv)
-        for core in (0, 1):
-            for k in (0, 1):
-
-                def go(i, _):
-                    chip = lax.rem(me // 2 + STRIDE * i, n // 2)
-                    peer = chip * 2 + core
-
-                    @pl.when(peer != me)
-                    def _():
-                        row_copy(k, s, peer, land, f_send, f_recv).start()
-
-                    return 0
-
-                lax.fori_loop(0, n // 2, go, 0)
 
     fill(0)
     pl.semaphore_wait(barrier, n + 1)
-    dispatch(0)
+    for q in range(4):
+        forward_part(q, 0)
     for s in range(1, slots):
         fill(s)
-        dispatch(s)
     lax.fori_loop(0, slots, compute, 0)
 
     spots = slots * rows
@@ -301,6 +349,9 @@
         for s in range(slots):
             loads[s].wait()
 
+    for s in range(slots - 1):
+        for item in range(3):
+            ring_end(item, s)
     fetch(0)
 
     def combine(j, sums):
@@ -337,12 +388,36 @@
         for item in range(3):
             own_copy(item, s).wait()
             for side in (0, 1):
-                for step in (1, 2):
-                    ring_copy(item, s, step, side).wait_recv()
+                if s == slots - 1:
+                    for step in (1, 2):
+                        ring_copy(item, s, step, side).wait_recv()
                 for step in range(3):
                     ring_copy(item, s, step, side).wait_send()
         for k in (0, 1):
             wait_send(k, s, b_send)
+
+
+def finish(slots, own_w, got_w, own_d, got_d, lo, dt, dg, gate, up, down, lo_out, dt_out, dg_out):
+    lo_out[...] = lo[...]
+    dt_out[...] = dt[...]
+    dg_out[...] = dg[...]
+    last = pl.program_id(0) == slots - 1
+    jobs = (
+        (own_w.at[0, 0], got_w.at[0, 0, 0], got_w.at[0, 1, 0], gate.at[0]),
+        (own_w.at[1, 0], got_w.at[1, 0, 0], got_w.at[1, 1, 0], up.at[0]),
+        (own_d.at[0], got_d.at[0, 0], got_d.at[1, 0], down.at[0]),
+    )
+
+    @pl.when(last)
+    def _():
+        for own, one, two, out in jobs:
+            both = one[...].astype(F32) + two[...].astype(F32)
+            out[...] = (own[...].astype(F32) + both).astype(BF16)
+
+    @pl.when(jnp.logical_not(last))
+    def _():
+        for own, _, _, out in jobs:
+            out[...] = own[...]
 
 
 def on_device(n, ring, tokens, expert_ids, gate_weights, slot_of_expert, w_gate, w_up, w_down, d_out):
@@ -393,6 +468,8 @@
             pltpu.VMEM((slots, ring, ff, chunk), BF16),
             pltpu.VMEM((2, slots, 2, chunk // 2, ff), BF16),
             pltpu.VMEM((slots, 2, ff // 2, chunk), BF16),
+            pltpu.VMEM((2, chunk, ff), BF16),
+            pltpu.VMEM((2, ff, chunk), BF16),
             pltpu.SemaphoreType.DMA((2, slots)),
             pltpu.SemaphoreType.DMA((2, slots)),
             pltpu.SemaphoreType.DMA((2, slots)),
@@ -402,6 +479,7 @@
             pltpu.SemaphoreType.DMA((slots, 3, 3, 2)),
             pltpu.SemaphoreType.DMA((2, slots)),
             pltpu.SemaphoreType.DMA((slots, 3)),
+            pltpu.SemaphoreType.DMA((2,)),
         ],
         compiler_params=pltpu.CompilerParams(
             collective_id=0, has_side_effects=True, vmem_limit_bytes=63 * 1024 * 1024
@@ -409,13 +487,38 @@
     )(gates_pos, tokens, d_out, w_gate, w_up, w_down)
     layer_out, d_tokens, d_gates, own_w, own_d, _, got_w, got_d = out
 
-    def total(own, got):
-        return (own.astype(F32) + got[0].astype(F32) + got[1].astype(F32)).astype(BF16)
-
-    return (
-        layer_out, d_tokens, d_gates.T,
-        total(own_w[0], got_w[0]), total(own_w[1], got_w[1]), total(own_d, got_d),
-    )
+    parts = 4
+    w_rows, d_rows, t_rows = chunk // parts, ff // parts, tok_rows // (parts * slots)
+
+    def late(s, j):
+        return jnp.where(s == slots - 1, j, 0)
+
+    w_out = pl.BlockSpec((1, w_rows, ff), lambda s, j: (s, j, 0))
+    d_out_spec = pl.BlockSpec((1, d_rows, chunk), lambda s, j: (s, j, 0))
+    t_spec = pl.BlockSpec((t_rows, width), lambda s, j: (s * parts + j, 0))
+    g_spec = pl.BlockSpec((tops, tok_rows), lambda s, j: (0, 0))
+    grad_gate, grad_up, grad_down, layer_out, d_tokens, d_gates = pl.pallas_call(
+        functools.partial(finish, slots),
+        grid=(slots, parts),
+        out_shape=[
+            jax.ShapeDtypeStruct((slots, chunk, ff), BF16),
+            jax.ShapeDtypeStruct((slots, chunk, ff), BF16),
+            jax.ShapeDtypeStruct((slots, ff, chunk), BF16),
+            jax.ShapeDtypeStruct((tok_rows, width), BF16),
+            jax.ShapeDtypeStruct((tok_rows, width), BF16),
+            jax.ShapeDtypeStruct((tops, tok_rows), F32),
+        ],
+        in_specs=[
+            pl.BlockSpec((2, 1, w_rows, ff), lambda s, j: (0, s, j, 0)),
+            pl.BlockSpec((2, 2, 1, w_rows, ff), lambda s, j: (0, 0, slots - 1, late(s, j), 0)),
+            d_out_spec,
+            pl.BlockSpec((2, 1, d_rows, chunk), lambda s, j: (0, slots - 1, late(s, j), 0)),
+            t_spec, t_spec, g_spec,
+        ],
+        out_specs=[w_out, w_out, d_out_spec, t_spec, t_spec, g_spec],
+        compiler_params=pltpu.CompilerParams(vmem_limit_bytes=63 * 1024 * 1024),
+    )(own_w, got_w, own_d, got_d, layer_out, d_tokens, d_gates)
+    return layer_out, d_tokens, d_gates.T, grad_gate, grad_up, grad_down
 
 
 def solution(mesh):

time: 219 us -> 217 us (level)
  other arithmetic: 10.3 us -> 2.16 us
  Pallas kernels: 205 us -> 213 us
    pallas_call x0 -> x1, Pallas kernels: none -> 8.72 us  [on_device(): pl.pallas_call(functools.partial(finish, slots), grid=(slots, parts), out...]
    convert_element_type x2 -> x0, other arithmetic: 8.18 us -> none  [total(): (own.astype(F32) + got[0].astype(F32) + got[1].astype(F32)).astype(BF16)]
where the time goes in v4:
time: 217 us; the launch traced here: 216 us
  Pallas kernels  213 us (98%)
    pallas_call x1, Pallas kernels, on_device(): pl.pallas_call(functools.partial(kernel, n, ring), out_shape=[jax.ShapeDt...  204 us
    pallas_call x1, Pallas kernels, on_device(): pl.pallas_call(functools.partial(finish, slots), grid=(slots, parts), out...  8.72 us

profile of v4, /device:TPU:1, one launch (start us, length us, event | category | flops | bytes accessed | tf_op | source)
XLA Modules:
  0.0 216.1 jit_solution(3502750030518410810)
XLA Ops:
  0.6 0.8 select_reduce_fusion.1
  1.4 0.1 fusion.1
  1.7 1.3 pad_maximum_fusion.gates_pos
  2.9 204.5 %shard_map.127 = (bf16[128,2048]{1,0:T(8,128)(2,1)}, bf16[128,2048]{1,0:T(8,128)(2,1)}, f32[4,128]{1,0:T(4,128)}, bf16[2,2,512,768]{3,2,1,0:T(8,128)(2,1)}, bf16...) custom-call(f32[8,128]{1,0:T(8,128)} %pad_maximum_fusion.gates_pos, ...), custom_call_target="tpu_custom_call" | custom-call | tf_op jit(solution)/shard_map/pallas_call | solution.py:445
  207.4 8.7 %shard_map.128 = (bf16[2,512,768]{2,1,0:T(8,128)(2,1)}, bf16[2,512,768]{2,1,0:T(8,128)(2,1)}, bf16[2,768,512]{2,1,0:T(8,128)(2,1)}, bf16[128,2048]{1,0:T(8,128)(...) custom-call(bf16[2,2,512,768]{3,2,1,0:T(8,128)(2,1)} %get-tuple-element.19.own_w, ...), custom_call_target="tpu_custom_call" | custom-call | tf_op jit(solution)/shard_map/pallas_call | solution.py:500
  (3 shorter events, 0.1 us)

commit v5 on v4

--- a/solution.py
+++ b/solution.py
@@ -487,7 +487,7 @@
     )(gates_pos, tokens, d_out, w_gate, w_up, w_down)
     layer_out, d_tokens, d_gates, own_w, own_d, _, got_w, got_d = out
 
-    parts = 4
+    parts = 2
     w_rows, d_rows, t_rows = chunk // parts, ff // parts, tok_rows // (parts * slots)
 
     def late(s, j):

time: 217 us -> 215 us (level)
  no operation moved by 1% of the time
where the time goes in v5:
time: 215 us
  Pallas kernels  212 us (99%)
  other arithmetic  2.16 us (1%)
    pallas_call x1, Pallas kernels, on_device(): pl.pallas_call(functools.partial(kernel, n, ring), out_shape=[jax.ShapeDt...  204 us
    pallas_call x1, Pallas kernels, on_device(): pl.pallas_call(functools.partial(finish, slots), grid=(slots, parts), out...  7.25 us

profile of v5, /device:TPU:1, one launch (start us, length us, event | category | flops | bytes accessed | tf_op | source)
XLA Modules:
  0.0 214.7 jit_solution(1093398569781971710)
XLA Ops:
  0.6 0.8 select_reduce_fusion.1
  1.4 0.1 fusion.1
  1.7 1.3 pad_maximum_fusion.gates_pos
  2.9 204.5 %shard_map.127 = (bf16[128,2048]{1,0:T(8,128)(2,1)}, bf16[128,2048]{1,0:T(8,128)(2,1)}, f32[4,128]{1,0:T(4,128)}, bf16[2,2,512,768]{3,2,1,0:T(8,128)(2,1)}, bf16...) custom-call(f32[8,128]{1,0:T(8,128)} %pad_maximum_fusion.gates_pos, ...), custom_call_target="tpu_custom_call" | custom-call | tf_op jit(solution)/shard_map/pallas_call | solution.py:445
  207.4 7.2 %shard_map.128 = (bf16[2,512,768]{2,1,0:T(8,128)(2,1)}, bf16[2,512,768]{2,1,0:T(8,128)(2,1)}, bf16[2,768,512]{2,1,0:T(8,128)(2,1)}, bf16[128,2048]{1,0:T(8,128)(...) custom-call(bf16[2,2,512,768]{3,2,1,0:T(8,128)(2,1)} %get-tuple-element.19.own_w, ...), custom_call_target="tpu_custom_call" | custom-call | tf_op jit(solution)/shard_map/pallas_call | solution.py:500
  (3 shorter events, 0.1 us)
